TPU v7x, 32 devices: a whole 2x2x4 slice. The times are simulated.
32 devices in a mesh: mask: 2 (over x), gx: 16 (over z, y, core).
Axes of the slice: x: 2, y: 2, z: 4, core: 2. Of those that a mesh axis runs over, the one named last changes fastest.
Arguments:
- e_field: float32 [3, 192, 24, 768], P(None, ('mask', 'gx')), parts along dimension 1, may hold values from -6 to 6
- h_field: float32 [3, 192, 24, 768], P(None, ('mask', 'gx')), parts along dimension 1, may hold values from -6 to 6
- polar: float32 [3, 192, 24, 768], P(None, ('mask', 'gx')), parts along dimension 1, may hold values from -6 to 6
- current: float32 [3, 192, 24, 768], P(None, ('mask', 'gx')), parts along dimension 1, may hold values from -6 to 6
- psi_h: float32 [2, 192, 6, 768], P(None, ('mask', 'gx')), parts along dimension 1, may hold values from -6 to 6
- psi_e: float32 [2, 192, 6, 768], P(None, ('mask', 'gx')), parts along dimension 1, may hold values from -6 to 6
- material: int32 [192, 24, 768], P(('mask', 'gx')), parts along dimension 0, may hold values from 0 to 3, as said below
- inv_eps_table: float32 [4], replicated, may hold values from 0.3 to 1
- decay_table: float32 [4], replicated, may hold values from 0.3 to 0.95
- drive_table: float32 [4], replicated, may hold values from 0.1 to 0.5
- strength_table: float32 [4], replicated, may hold values from 0.2 to 1
- spring_table: float32 [4], replicated, may hold values from 0.05 to 1
- orders: int32 [2, 4096], replicated, may hold values from -32 to 31
Outputs:
- e_out: float32 [3, 192, 24, 768], P(None, ('mask', 'gx')), parts along dimension 1
- h_out: float32 [3, 192, 24, 768], P(None, ('mask', 'gx')), parts along dimension 1
- polar_out: float32 [3, 192, 24, 768], P(None, ('mask', 'gx')), parts along dimension 1
- current_out: float32 [3, 192, 24, 768], P(None, ('mask', 'gx')), parts along dimension 1
- psi_h_out: float32 [2, 192, 6, 768], P(None, ('mask', 'gx')), parts along dimension 1
- psi_e_out: float32 [2, 192, 6, 768], P(None, ('mask', 'gx')), parts along dimension 1
- pupil: float32 [4, 8192], P(None, 'mask'), parts along dimension 1
There are 2 independent parts, one for each index of `mask`. A program takes and returns all parts, laid end to end along the dimension named above; an argument that names none is the same for every part. Nothing has to cross between parts.
Inputs may be any that keep to these rules, and one draw needn't show every extreme that they name: `material`: 0 is vacuum, 1 absorber, 2 molybdenum, 3 silicon.
All inputs are finite; a program needn't handle non-finite values.
Results may differ from a plain program's by a relative error of at most 0.000082.
Values sent between devices are 32-bit elements; how exact they have to be, the bound alone decides.
A program may use at most 64 MiB of HBM per device.

v0:
```python
import math

import jax
import jax.numpy as jnp
from jax import lax
from jax.sharding import PartitionSpec as P

NPML = 6
KSPAN = 64
STEPS = 4


COURANT = 0.5
SIGMA_MAX = 0.8
PML_ALPHA = 0.05


def passed_along(value, axis, steps):
    count = lax.axis_size(axis)
    pairs = [(source, (source + steps) % count) for source in range(count)]
    return lax.ppermute(value, axis, pairs)


def z_forward(field):
    after = jnp.concatenate([field[..., 1:, :], jnp.zeros_like(field[..., :1, :])], axis=-2)
    return after - field


def z_backward(field):
    before = jnp.concatenate([jnp.zeros_like(field[..., :1, :]), field[..., :-1, :]], axis=-2)
    return field - before


def y_forward(field):
    return jnp.roll(field, -1, axis=-1) - field


def y_backward(field):
    return field - jnp.roll(field, 1, axis=-1)


def pad_rows(memory, total):
    return jnp.pad(memory, ((0, 0), (0, total - memory.shape[-2]), (0, 0)))


def pml_coefficients(layers, offset):
    depth = (layers - jnp.arange(layers, dtype=jnp.float32) - offset) / layers
    sigma = SIGMA_MAX * depth**3
    decay = jnp.exp(-(sigma + PML_ALPHA))
    gain = sigma / (sigma + PML_ALPHA) * (decay - 1.0)
    return (decay[:, None], gain[:, None])


def lookup(material, table):
    total = jnp.zeros(material.shape, table.dtype)
    for index in range(table.shape[0]):
        total = total + jnp.where(material == index, table[index], 0.0)
    return total


def h_update(e_x, e_y, e_z, ey_ahead, ez_ahead, h_x, h_y, h_z, psi_hx, psi_hy, decay, gain):
    layers = psi_hx.shape[-2]
    depth_cells = e_x.shape[-2]
    dey_dz = z_forward(e_y)
    dex_dz = z_forward(e_x)
    psi_hx_new = decay * psi_hx + gain * dey_dz[:, :layers]
    psi_hy_new = decay * psi_hy + gain * dex_dz[:, :layers]
    hx_new = h_x - COURANT * (y_forward(e_z) - dey_dz - pad_rows(psi_hx_new, depth_cells))
    hy_new = h_y - COURANT * (dex_dz + pad_rows(psi_hy_new, depth_cells) - (ez_ahead - e_z))
    hz_new = h_z - COURANT * (ey_ahead - e_y - y_forward(e_x))
    return (hx_new, hy_new, hz_new, psi_hx_new, psi_hy_new)


def e_update(
    hx_new,
    hy_new,
    hz_new,
    hy_behind,
    hz_behind,
    psi_ex,
    psi_ey,
    decay,
    gain,
    e_field,
    polar,
    current,
    coefs,
):
    inv_eps, decay_j, drive_j, strength, spring = coefs
    layers = psi_ex.shape[-2]
    depth_cells = hx_new.shape[-2]
    dhy_dz = z_backward(hy_new)
    dhx_dz = z_backward(hx_new)
    psi_ex_new = decay * psi_ex + gain * dhy_dz[:, :layers]
    psi_ey_new = decay * psi_ey + gain * dhx_dz[:, :layers]
    curl_x = y_backward(hz_new) - (dhy_dz + pad_rows(psi_ex_new, depth_cells))
    curl_y = dhx_dz + pad_rows(psi_ey_new, depth_cells) - (hz_new - hz_behind)
    curl_z = hy_new - hy_behind - y_backward(hx_new)
    curl = jnp.stack([curl_x, curl_y, curl_z])
    current_new = decay_j * current + drive_j * (strength * e_field - spring * polar)
    polar_new = polar + current_new
    e_new = e_field + inv_eps * (COURANT * curl - current_new)
    return (e_new, polar_new, current_new, psi_ex_new, psi_ey_new)


def y_table(cells, span):
    rows = jnp.arange(cells, dtype=jnp.int32)
    waves = jnp.arange(span, dtype=jnp.int32) - span // 2
    phase = (rows[:, None] * waves[None, :] % cells).astype(jnp.float32) * (2.0 * math.pi / cells)
    return jnp.concatenate([jnp.cos(phase), jnp.sin(phase)], axis=1)


def x_table(rows, cells, span):
    waves = jnp.arange(span, dtype=jnp.int32) - span // 2
    phase = (rows[:, None] * waves[None, :] % cells).astype(jnp.float32) * (2.0 * math.pi / cells)
    return (jnp.cos(phase), jnp.sin(phase))


def local_spectrum(plane, rows, cells_x, span):
    comps, planes, cells_y = plane.shape
    highest = lax.Precision.HIGHEST
    table = y_table(cells_y, span)
    mixed = jnp.dot(
        plane.reshape(comps * planes, cells_y),
        table,
        precision=highest,
        preferred_element_type=jnp.float32,
    )
    mixed = mixed.reshape(comps, planes, 2, span)
    real_y = mixed[:, :, 0]
    imag_y = -mixed[:, :, 1]
    cos_x, sin_x = x_table(rows, cells_x, span)
    real = jnp.einsum("cxk,xj->cjk", real_y, cos_x, precision=highest) + jnp.einsum(
        "cxk,xj->cjk", imag_y, sin_x, precision=highest
    )
    imag = jnp.einsum("cxk,xj->cjk", imag_y, cos_x, precision=highest) - jnp.einsum(
        "cxk,xj->cjk", real_y, sin_x, precision=highest
    )
    return jnp.stack([real, imag], axis=1)


def pick_orders(spectrum, orders, cells_total):
    span = spectrum.shape[-1]
    flat = spectrum.reshape(4, span * span) / math.sqrt(cells_total)
    index = (orders[0] + span // 2) * span + (orders[1] + span // 2)
    return jnp.take(flat, index, axis=1)


def shards(
    e_field,
    h_field,
    polar,
    current,
    psi_h,
    psi_e,
    material,
    inv_eps_table,
    decay_table,
    drive_table,
    strength_table,
    spring_table,
    orders,
):
    planes = e_field.shape[1]
    layers = psi_h.shape[2]
    coefs = tuple(
        (
            lookup(material, table)
            for table in (inv_eps_table, decay_table, drive_table, strength_table, spring_table)
        )
    )
    decay_h, gain_h = pml_coefficients(layers, 0.5)
    decay_e, gain_e = pml_coefficients(layers, 0.0)
    for step in range(STEPS):
        e_x, e_y, e_z = (e_field[0], e_field[1], e_field[2])
        front = passed_along(e_field[1:3, 0], "gx", -1)
        ey_ahead = jnp.concatenate([e_y[1:], front[0:1]], axis=0)
        ez_ahead = jnp.concatenate([e_z[1:], front[1:2]], axis=0)
        hx_new, hy_new, hz_new, psi_hx, psi_hy = h_update(
            e_x,
            e_y,
            e_z,
            ey_ahead,
            ez_ahead,
            h_field[0],
            h_field[1],
            h_field[2],
            psi_h[0],
            psi_h[1],
            decay_h,
            gain_h,
        )
        sent = passed_along(jnp.stack([hy_new[planes - 1], hz_new[planes - 1]]), "gx", 1)
        hy_edge, hz_edge = (sent[0:1], sent[1:2])
        hy_behind = jnp.concatenate([hy_edge, hy_new[:-1]], axis=0)
        hz_behind = jnp.concatenate([hz_edge, hz_new[:-1]], axis=0)
        h_field = jnp.stack([hx_new, hy_new, hz_new])
        psi_h = jnp.stack([psi_hx, psi_hy])
        e_field, polar, current, psi_ex, psi_ey = e_update(
            hx_new,
            hy_new,
            hz_new,
            hy_behind,
            hz_behind,
            psi_e[0],
            psi_e[1],
            decay_e,
            gain_e,
            e_field,
            polar,
            current,
            coefs,
        )
        psi_e = jnp.stack([psi_ex, psi_ey])
    total_x = planes * lax.axis_size("gx")
    rows = lax.axis_index("gx") * planes + jnp.arange(planes, dtype=jnp.int32)
    partial_spectrum = local_spectrum(e_field[0:2, :, NPML, :], rows, total_x, KSPAN)
    spectrum = lax.psum(partial_spectrum, "gx")
    pupil = pick_orders(spectrum, orders, total_x * e_field.shape[3])
    return (e_field, h_field, polar, current, psi_h, psi_e, pupil)


def solution(mesh):
    in_specs = (
        P(None, ("mask", "gx"), None, None),
        P(None, ("mask", "gx"), None, None),
        P(None, ("mask", "gx"), None, None),
        P(None, ("mask", "gx"), None, None),
        P(None, ("mask", "gx"), None, None),
        P(None, ("mask", "gx"), None, None),
        P(("mask", "gx"), None, None),
        P(),
        P(),
        P(),
        P(),
        P(),
        P(),
    )
    out_specs = (
        P(None, ("mask", "gx"), None, None),
        P(None, ("mask", "gx"), None, None),
        P(None, ("mask", "gx"), None, None),
        P(None, ("mask", "gx"), None, None),
        P(None, ("mask", "gx"), None, None),
        P(None, ("mask", "gx"), None, None),
        P(None, "mask"),
    )
    return jax.shard_map(shards, mesh=mesh, in_specs=in_specs, out_specs=out_specs, check_vma=False)
```

profile of v0, /device:TPU:0, one launch (start us, length us, event | category | flops | bytes accessed | tf_op | source)
XLA Modules:
  0.0 212.8 jit_solution(3916744526809756581)
XLA Ops:
  7.2 0.9 slice_bitcast_fusion.19
  8.1 5.5 %collective-permute-start = (f32[2,24,768]{2,1,0:T(8,128)S(1)}, f32[2,24,768]{2,1,0:T(8,128)S(1)}, u32[]{:S(2)}, u32[]{:S(2)}) collective-permute-start(f32[2,24,768]{2,1,0:T(8,128)S(1)} %slice_bitcast_fusion.19), channel_id=1, source_target_pairs={{0,15},{1,0},{2,1},{3,2},{4,3},{5,4},{6,5},{7,6},{8,7},{9,8},{10,9... | collective-permute-start | bytes 442376 | tf_op jit(solution)/shard_map/ppermute | solution.py:21
  13.6 1.4 slice_bitcast_fusion.3
  15.3 0.9 slice_bitcast_fusion.38
  16.7 0.8 fusion.182
  17.9 0.9 fusion.183
  18.7 0.6 fusion.193
  19.4 0.6 fusion.192
  20.0 0.7 fusion.189
  20.6 0.7 fusion.191
  21.3 0.7 fusion.190
  22.0 1.6 fusion.96
  23.6 0.6 compare_select_fusion
  24.4 0.9 copy-done.23
  25.3 2.9 %select_add_fusion.4 = (f32[6,24,768]{2,1,0:T(8,128)S(1)}, pred[6,24,768]{2,1,0:T(8,128)(4,1)S(1)}, pred[6,24,768]{2,1,0:T(8,128)(4,1)S(1)}, pred[6,24,768]{2,1,0:T(8,128)(4,1)S(1)}, pred[6,24,768]{2,1,0:T(8,128)(4,1)S(1)}) fusion(f32[]{:T(128)} %bitcast.3, f32[]{:T(128)} %bitcast.2, f32[]{:T(128)} %bitcast.1, f32[]{:T(128)} %bitcast, ...), kind=kLoop, calls=%fused_computation.169 | loop fusion | flops 1216512 | bytes 1327120 | tf_op jit(solution)/shard_map/add | solution.py:57
  28.3 2.6 %select_add_fusion = f32[6,24,768]{2,1,0:T(8,128)S(1)} fusion(pred[6,24,768]{2,1,0:T(8,128)(4,1)S(1)} %get-tuple-element.46, pred[6,24,768]{2,1,0:T(8,128)(4,1)S(1)} %get-tuple-element.45, pred[6,24,768]{2,1,0:T(8,128)(4,1)S(1)} %get-tuple-element.44, pred[6,24,768]{2,1,0:T(8,128)(4,1)S(1)} %get-tuple-element.43, f32[]{:T(128)} %bitcast.35, f32[]{:T(128)} %bitcast.34, ...), kind=kLoop, calls=%fused_computation.160 | loop fusion | flops 774144 | bytes 884752 | tf_op jit(solution)/shard_map/add | solution.py:57
  30.9 9.1 %select_add_fusion.3 = (f32[6,24,768]{2,1,0:T(8,128)}, f32[6,24,768]{2,1,0:T(8,128)}, f32[6,24,768]{2,1,0:T(8,128)}) fusion(pred[6,24,768]{2,1,0:T(8,128)(4,1)S(1)} %get-tuple-element.46, pred[6,24,768]{2,1,0:T(8,128)(4,1)S(1)} %get-tuple-element.45, pred[6,24,768]{2,1,0:T(8,128)(4,1)S(1)} %get-tuple-element.44, ...), kind=kLoop, calls=%fused_computation.163 | loop fusion | flops 2322432 | bytes 1769520 | tf_op jit(solution)/shard_map/add | solution.py:57
  40.1 0.6 slice_bitcast_fusion.29
  40.7 0.6 slice_bitcast_fusion.30
  41.8 0.7 pad_maximum_fusion.4
  42.7 7.3 %collective-permute-done.1 = f32[2,24,768]{2,1,0:T(8,128)} collective-permute-done((f32[2,24,768]{2,1,0:T(8,128)}, f32[2,24,768]{2,1,0:T(8,128)}, u32[]{:S(2)}, u32[]{:S(2)}) %collective-permute-start.1) | collective-permute-done | bytes 147488 | tf_op jit(solution)/shard_map/ppermute | solution.py:21
  50.1 0.9 fusion.188
  51.3 0.6 copy-done.21
  52.4 0.9 copy-done.14
  54.0 0.6 fusion.2
  55.5 0.7 copy-done.13
  56.3 1.7 collective-permute-done.2
  58.5 0.5 copy-done.11
  60.0 6.9 %collective-permute-done.3 = f32[2,24,768]{2,1,0:T(8,128)S(1)} collective-permute-done((f32[2,24,768]{2,1,0:T(8,128)S(1)}, f32[2,24,768]{2,1,0:T(8,128)S(1)}, u32[]{:S(2)}, u32[]{:S(2)}) %collective-permute-start.3) | collective-permute-done | bytes 147488 | tf_op jit(solution)/shard_map/ppermute | solution.py:21
  67.6 0.7 fusion.5
  69.2 2.4 %collective-permute-done.4 = f32[2,24,768]{2,1,0:T(8,128)S(1)} collective-permute-done((f32[2,24,768]{2,1,0:T(8,128)S(1)}, f32[2,24,768]{2,1,0:T(8,128)S(1)}, u32[]{:S(2)}, u32[]{:S(2)}) %collective-permute-start.4) | collective-permute-done | bytes 147488 | tf_op jit(solution)/shard_map/ppermute | solution.py:21
  73.5 6.7 %collective-permute-done.5 = f32[2,24,768]{2,1,0:T(8,128)S(1)} collective-permute-done((f32[2,24,768]{2,1,0:T(8,128)S(1)}, f32[2,24,768]{2,1,0:T(8,128)S(1)}, u32[]{:S(2)}, u32[]{:S(2)}) %collective-permute-start.5) | collective-permute-done | bytes 147488 | tf_op jit(solution)/shard_map/ppermute | solution.py:21
  80.9 2.2 %fusion.14 = (f32[3,6,24,768]{3,2,1,0:T(8,128)}, f32[3,6,24,768]{3,2,1,0:T(8,128)S(1)}, f32[3,6,24,768]{3,2,1,0:T(8,128)S(1)}) fusion(f32[3,6,24,768]{3,2,1,0:T(8,128)S(1)} %copy-done.1, f32[3,6,24,768]{3,2,1,0:T(8,128)S(1)} %get-tuple-element.41, f32[6,24,768]{2,1,0:T(8,128)S(1)} %select_add_fusion, f32[3,6,24,768]{3,2,1,0:T(8,128)S(1)} %fusion.5, ...), kind=kLoop, calls=%fused_computation.28 | loop fusion | flops 9289728 | bytes 12828672 | tf_op jit(solution)/shard_map/add | solution.py:101
  84.0 2.5 %collective-permute-done.6 = f32[2,24,768]{2,1,0:T(8,128)S(1)} collective-permute-done((f32[2,24,768]{2,1,0:T(8,128)S(1)}, f32[2,24,768]{2,1,0:T(8,128)S(1)}, u32[]{:S(2)}, u32[]{:S(2)}) %collective-permute-start.6) | collective-permute-done | bytes 147488 | tf_op jit(solution)/shard_map/ppermute | solution.py:21
  87.3 0.7 copy-done.7
  88.2 1.7 fusion.84
  90.2 0.9 copy.180
  91.0 1.2 pad_maximum_fusion
  92.2 2.6 %collective-permute-done.7 = f32[2,24,768]{2,1,0:T(8,128)S(1)} collective-permute-done((f32[2,24,768]{2,1,0:T(8,128)S(1)}, f32[2,24,768]{2,1,0:T(8,128)S(1)}, u32[]{:S(2)}, u32[]{:S(2)}) %collective-permute-start.7) | collective-permute-done | bytes 147488 | tf_op jit(solution)/shard_map/ppermute | solution.py:21
  96.4 0.6 fusion.118
  98.6 0.7 pad_maximum_fusion.8
  99.4 0.9 copy.181
  100.2 85.0 %all-reduce.34.cloned.1.call-done = f32[2,2,64,64]{3,2,0,1:T(8,128)} async-done(((f32[2,2,64,64]{3,2,0,1:T(8,128)}), f32[2,2,64,64]{3,2,0,1:T(8,128)}) %all-reduce.34.cloned.1.call-update) | async-done | bytes 65552 | tf_op jit(solution)/shard_map/psum | solution.py:218
  185.2 0.9 broadcast_multiply_fusion
  186.2 0.6 copy.179
  186.9 14.2 %gather_fusion = f32[4096,4]{1,0:T(8,128)} fusion(f32[4,4096]{0,1:T(8,128)S(1)} %copy.179, s32[4096]{0:T(1024)S(1)} %broadcast_clamp_fusion), kind=kCustom, calls=%fused_computation | custom fusion | bytes 147456 | tf_op jit(solution)/shard_map/jit(_take)/gather | solution.py:146
  201.1 3.6 %select_bitcast_fusion = f32[4,4096]{0,1:T(8,128)S(1)} fusion(f32[4096,4]{1,0:T(8,128)} %gather_fusion, pred[4096]{0:T(1024)(128)(4,1)S(1)} %compare_and_fusion), kind=kLoop, calls=%fused_computation.1 | loop fusion | flops 16384 | bytes 135168 | tf_op jit(solution)/shard_map/jit(_take)/select_n | solution.py:146
  204.7 1.2 copy.182
  (199 shorter events, 15.1 us)
Async XLA Ops:
  7.2 178.0 %all-reduce.34.cloned.1.call-start = ((), (), s32[]{:S(2)}) async-start(), calls=%async_computation | async-start | bytes 262144 | tf_op jit(solution)/shard_map/psum | solution.py:218
  8.1 32.5 %collective-permute-start = (f32[2,24,768]{2,1,0:T(8,128)S(1)}, f32[2,24,768]{2,1,0:T(8,128)S(1)}, u32[]{:S(2)}, u32[]{:S(2)}) collective-permute-start(f32[2,24,768]{2,1,0:T(8,128)S(1)} %slice_bitcast_fusion.19), channel_id=1, source_target_pairs={{0,15},{1,0},{2,1},{3,2},{4,3},{5,4},{6,5},{7,6},{8,7},{9,8},{10,9... | collective-permute-start | bytes 442376 | tf_op jit(solution)/shard_map/ppermute | solution.py:21
  15.2 1.5 copy-start
  15.2 12.9 %copy-start.30 = (f32[6]{0:T(128)}, f32[6]{0:T(128)S(1)}, u32[]{:S(2)}) copy-start(f32[6]{0:T(128)S(1)} %get-tuple-element.180) | copy-start | bytes 76
  15.3 12.9 %copy-start.32 = (f32[6]{0:T(128)}, f32[6]{0:T(128)S(1)}, u32[]{:S(2)}) copy-start(f32[6]{0:T(128)S(1)} %get-tuple-element.181) | copy-start | bytes 76
  16.7 1.0 copy-start.26
  16.7 1.2 copy-start.27
  17.5 1.2 copy-start.36
  17.5 1.8 copy-start.37
  17.5 2.4 %copy-start.38 = (f32[4]{0:T(128)S(1)}, f32[4]{0:T(128)}, u32[]{:S(2)}) copy-start(f32[4]{0:T(128)} %param.21) | copy-start | bytes 52
  17.5 3.1 %copy-start.39 = (f32[4]{0:T(128)S(1)}, f32[4]{0:T(128)}, u32[]{:S(2)}) copy-start(f32[4]{0:T(128)} %param.23) | copy-start | bytes 52
  17.5 3.8 %copy-start.40 = (f32[4]{0:T(128)S(1)}, f32[4]{0:T(128)}, u32[]{:S(2)}) copy-start(f32[4]{0:T(128)} %param.22) | copy-start | bytes 52
  17.5 6.0 %copy-start.29 = (s32[2,4096]{1,0:T(2,128)S(1)}, s32[2,4096]{1,0:T(2,128)}, u32[]{:S(2)}) copy-start(s32[2,4096]{1,0:T(2,128)} %param.25) | copy-start | bytes 98308
  17.6 6.0 %copy-start.34 = (s32[64]{0:T(128)}, s32[64]{0:T(128)S(1)}, u32[]{:S(2)}) copy-start(s32[64]{0:T(128)S(1)} %iota_add_fusion) | copy-start | bytes 772
  24.2 1.0 copy-start.23
  28.3 13.0 %copy-start.10 = (f32[6,6,768]{2,1,0:T(8,128)}, f32[6,6,768]{2,1,0:T(8,128)S(1)}, u32[]{:S(2)}) copy-start(f32[6,6,768]{2,1,0:T(8,128)S(1)} %get-tuple-element.157) | copy-start | bytes 331780
  28.3 13.0 %copy-start.12 = (f32[6,6,768]{2,1,0:T(8,128)}, f32[6,6,768]{2,1,0:T(8,128)S(1)}, u32[]{:S(2)}) copy-start(f32[6,6,768]{2,1,0:T(8,128)S(1)} %get-tuple-element.156) | copy-start | bytes 331780
  30.9 10.4 %copy-start.6 = (f32[3,6,24,768]{3,2,1,0:T(8,128)S(1)}, f32[3,6,24,768]{3,2,1,0:T(8,128)}, u32[]{:S(2)}) copy-start(f32[3,6,24,768]{3,2,1,0:T(8,128)} %param.14) | copy-start | bytes 3981316
  42.5 7.6 %collective-permute-start.1 = (f32[2,24,768]{2,1,0:T(8,128)}, f32[2,24,768]{2,1,0:T(8,128)}, u32[]{:S(2)}, u32[]{:S(2)}) collective-permute-start(f32[2,24,768]{2,1,0:T(8,128)} %pad_maximum_fusion.4), channel_id=1, source_target_pairs={{0,1},{1,2},{2,3},{3,4},{4,5},{5,6},{6,7},{7,8},{8,9},{9,10},{10,1... | collective-permute-start | bytes 442376 | tf_op jit(solution)/shard_map/ppermute | solution.py:21
  51.0 0.9 copy-start.21
  51.0 0.9 copy-start.22
  51.9 1.3 copy-start.14
  52.1 1.6 copy-start.1
  52.1 1.7 copy-start.2
  52.1 1.8 copy-start.3
  52.1 2.0 copy-start.4
  55.3 0.9 copy-start.13
  55.3 0.9 copy-start.31
  55.3 0.9 copy-start.33
  55.3 2.7 %collective-permute-start.2 = (f32[2,24,768]{2,1,0:T(8,128)S(1)}, f32[2,24,768]{2,1,0:T(8,128)S(1)}, u32[]{:S(2)}, u32[]{:S(2)}) collective-permute-start(f32[2,24,768]{2,1,0:T(8,128)S(1)} %slice_bitcast_fusion.18), channel_id=1, source_target_pairs={{0,15},{1,0},{2,1},{3,2},{4,3},{5,4},{6,5},{7,6},{8,7},{9,8},{10,9... | collective-permute-start | bytes 442376 | tf_op jit(solution)/shard_map/ppermute | solution.py:21
  58.1 0.9 copy-start.11
  59.1 0.7 copy-start.28
  59.3 7.6 %collective-permute-start.3 = (f32[2,24,768]{2,1,0:T(8,128)S(1)}, f32[2,24,768]{2,1,0:T(8,128)S(1)}, u32[]{:S(2)}, u32[]{:S(2)}) collective-permute-start(f32[2,24,768]{2,1,0:T(8,128)S(1)} %pad_maximum_fusion.5), channel_id=1, source_target_pairs={{0,1},{1,2},{2,3},{3,4},{4,5},{5,6},{6,7},{7,8},{8,9},{9,10},{10,1... | collective-permute-start | bytes 442376 | tf_op jit(solution)/shard_map/ppermute | solution.py:21
  68.9 2.7 %collective-permute-start.4 = (f32[2,24,768]{2,1,0:T(8,128)S(1)}, f32[2,24,768]{2,1,0:T(8,128)S(1)}, u32[]{:S(2)}, u32[]{:S(2)}) collective-permute-start(f32[2,24,768]{2,1,0:T(8,128)S(1)} %slice_bitcast_fusion.17), channel_id=1, source_target_pairs={{0,15},{1,0},{2,1},{3,2},{4,3},{5,4},{6,5},{7,6},{8,7},{9,8},{10,9... | collective-permute-start | bytes 442376 | tf_op jit(solution)/shard_map/ppermute | solution.py:21
  72.2 0.9 copy-start.19
  72.2 1.0 copy-start.20
  72.4 7.8 %collective-permute-start.5 = (f32[2,24,768]{2,1,0:T(8,128)S(1)}, f32[2,24,768]{2,1,0:T(8,128)S(1)}, u32[]{:S(2)}, u32[]{:S(2)}) collective-permute-start(f32[2,24,768]{2,1,0:T(8,128)S(1)} %pad_maximum_fusion.6), channel_id=1, source_target_pairs={{0,1},{1,2},{2,3},{3,4},{4,5},{5,6},{6,7},{7,8},{8,9},{9,10},{10,1... | collective-permute-start | bytes 442376 | tf_op jit(solution)/shard_map/ppermute | solution.py:21
  83.1 12.8 %copy-start.5 = (f32[3,6,24,768]{3,2,1,0:T(8,128)}, f32[3,6,24,768]{3,2,1,0:T(8,128)S(1)}, u32[]{:S(2)}) copy-start(f32[3,6,24,768]{3,2,1,0:T(8,128)S(1)} %get-tuple-element.38) | copy-start | bytes 3981316
  83.7 2.7 %collective-permute-start.6 = (f32[2,24,768]{2,1,0:T(8,128)S(1)}, f32[2,24,768]{2,1,0:T(8,128)S(1)}, u32[]{:S(2)}, u32[]{:S(2)}) collective-permute-start(f32[2,24,768]{2,1,0:T(8,128)S(1)} %slice_bitcast_fusion.16), channel_id=1, source_target_pairs={{0,15},{1,0},{2,1},{3,2},{4,3},{5,4},{6,5},{7,6},{8,7},{9,8},{10,9... | collective-permute-start | bytes 442376 | tf_op jit(solution)/shard_map/ppermute | solution.py:21
  87.0 1.0 copy-start.7
  87.0 1.1 copy-start.8
  87.0 1.1 copy-start.24
  87.1 1.1 copy-start.25
  87.2 7.6 %collective-permute-start.7 = (f32[2,24,768]{2,1,0:T(8,128)S(1)}, f32[2,24,768]{2,1,0:T(8,128)S(1)}, u32[]{:S(2)}, u32[]{:S(2)}) collective-permute-start(f32[2,24,768]{2,1,0:T(8,128)S(1)} %pad_maximum_fusion.7), channel_id=1, source_target_pairs={{0,1},{1,2},{2,3},{3,4},{4,5},{5,6},{6,7},{7,8},{8,9},{9,10},{10,1... | collective-permute-start | bytes 442376 | tf_op jit(solution)/shard_map/ppermute | solution.py:21
  96.0 1.1 copy-start.35
  96.3 89.8 %copy-start.9 = (f32[3,6,24,768]{3,2,1,0:T(8,128)}, f32[3,6,24,768]{3,2,1,0:T(8,128)S(1)}, u32[]{:S(2)}) copy-start(f32[3,6,24,768]{3,2,1,0:T(8,128)S(1)} %fusion.11) | copy-start | bytes 3981316
  96.4 2.9 %copy-start.16 = (f32[6,6,768]{2,1,0:T(8,128)S(1)}, f32[6,6,768]{2,1,0:T(8,128)}, u32[]{:S(2)}) copy-start(f32[6,6,768]{2,1,0:T(8,128)} %copy-done.15) | copy-start | bytes 331780
  96.4 2.9 %copy-start.18 = (f32[6,6,768]{2,1,0:T(8,128)S(1)}, f32[6,6,768]{2,1,0:T(8,128)}, u32[]{:S(2)}) copy-start(f32[6,6,768]{2,1,0:T(8,128)} %copy-done.17) | copy-start | bytes 331780
  (2 other events, 1.4 us)
Sparse Core Ops, SparseCore 0:
  99.4 85.7 all-reduce.33
where the time goes:
time: 215 us; the launch traced here: 213 us
  waiting for transfers between devices  115 us (53%)
  local copies, waits for them, and re-layouts  39 us (18%)
  other arithmetic  35.5 us (17%)
  between operations  15 us (7%)
  starting transfers between devices  6.06 us (3%)
    psum x1, waiting for transfers between devices, shards(): spectrum = lax.psum(partial_spectrum, 'gx')  85 us
    ppermute x8, waiting for transfers between devices, passed_along(): return lax.ppermute(value, axis, pairs)  30.1 us
    add x3, other arithmetic, lookup(): total = total + jnp.where(material == index, table[index], 0.0)  14.6 us
    gather x1, local copies, waits for them, and re-layouts, pick_orders(): return jnp.take(flat, index, axis=1)  14.2 us
    unnamed x85, local copies, waits for them, and re-layouts  10.3 us
    ppermute x8, starting transfers between devices, passed_along(): return lax.ppermute(value, axis, pairs)  6.03 us
  transfers between devices with their start and end apart: 9, of which 8 were waited for; matrix products, arithmetic and copies ran while one was open for 15% of the time, Pallas kernels for 0%

commit v1 on v0

v1 whole, which is shorter than its diff:
```python
import functools
import math

import jax
import jax.numpy as jnp
import numpy as np
from jax import lax
from jax.experimental import pallas as pl
from jax.experimental.pallas import tpu as pltpu
from jax.sharding import PartitionSpec as P

KSPAN = 64
STEPS = 4
COURANT = 0.5
SIGMA_MAX = 0.8
PML_ALPHA = 0.05
ROWS = 8
LANES = 128


def profile_table(layers):
    out = []
    for offset in (0.5, 0.0):
        depth = (layers - np.arange(layers, dtype=np.float64) - offset) / layers
        sigma = SIGMA_MAX * depth**3
        decay = np.exp(-(sigma + PML_ALPHA))
        gain = sigma / (sigma + PML_ALPHA) * (decay - 1.0)
        for values in (decay, gain):
            column = np.zeros((ROWS, 1))
            column[:layers, 0] = values
            out.append(np.broadcast_to(column, (ROWS, LANES)))
    return np.stack(out).astype(np.float32)


def wave_table(cells, span):
    rows = np.arange(cells, dtype=np.int64)
    waves = np.arange(span, dtype=np.int64) - span // 2
    phase = (rows[:, None] * waves[None, :] % cells) * (2.0 * math.pi / cells)
    return np.concatenate([np.cos(phase), np.sin(phase)], axis=1)


def x_matrix(count, planes, rows, span):
    waves = wave_table(count * planes, span).T.reshape(2 * span, count, planes)
    out = np.zeros((2, 2 * span, count, rows))
    for comp in range(2):
        out[comp, :, :, comp * planes : (comp + 1) * planes] = waves
    return out.reshape(4 * span, count * rows).astype(np.float32)


def kernel(
    count,
    layers,
    e_in,
    h_in,
    p_in,
    c_in,
    psi_h_in,
    psi_e_in,
    mat_in,
    ytab_in,
    xmat_in,
    inv_eps_table,
    decay_table,
    drive_table,
    strength_table,
    spring_table,
    prof,
    orders,
    e,
    h,
    pol,
    cur,
    psi_h_out,
    psi_e_out,
    pupil,
    mat,
    coefs,
    psi_h,
    psi_e,
    ahead,
    behind,
    halo,
    halo_psi,
    ytab,
    xmat,
    line,
    gathered,
    local_sem,
    left_send,
    left_recv,
    right_send,
    right_recv,
    first_send,
    first_recv,
    all_send,
    all_recv,
):
    planes, depth, cells = mat.shape
    tiles = depth // ROWS
    me = lax.axis_index("gx")
    right, left = lax.rem(me + 1, count), lax.rem(me + count - 1, count)

    barrier = pltpu.get_barrier_semaphore()

    def greet(k, carry):
        pl.semaphore_signal(
            barrier,
            inc=1,
            device_id={"gx": lax.rem(me + k, count)},
            device_id_type=pl.DeviceIdType.MESH,
        )
        return carry

    lax.fori_loop(1, count, greet, 0)
    loads = [
        pltpu.make_async_copy(source, target, local_sem.at[index])
        for index, (source, target) in enumerate(
            [
                (e_in, e),
                (h_in, h),
                (mat_in, mat),
                (c_in, cur),
                (p_in, pol),
                (ytab_in, ytab),
                (xmat_in, xmat),
            ]
        )
    ]
    for load in loads:
        load.start()

    row = lax.broadcasted_iota(jnp.int32, (ROWS, cells), 0)
    first_row = row == 0
    last_row = row == ROWS - 1

    def wide(index):
        return jnp.concatenate([prof[index]] * (cells // LANES), axis=1)

    def tile(ref, t):
        return ref[t * ROWS : (t + 1) * ROWS, :]

    def z_next(ref, t):
        moved = pltpu.roll(tile(ref, t), ROWS - 1, 0)
        if t == tiles - 1:
            return jnp.where(last_row, 0.0, moved)
        return jnp.where(last_row, ref[(t + 1) * ROWS : (t + 1) * ROWS + 1, :], moved)

    def z_prev(ref, t):
        moved = pltpu.roll(tile(ref, t), 1, 0)
        if t == 0:
            return jnp.where(first_row, 0.0, moved)
        return jnp.where(first_row, ref[t * ROWS - 1 : t * ROWS, :], moved)

    def y_next(value):
        return pltpu.roll(value, cells - 1, 1)

    def y_prev(value):
        return pltpu.roll(value, 1, 1)

    def h_plane(ex, ey, ez, ey2, ez2, hx, hy, hz, psx, psy):
        for t in range(tiles):
            at = slice(t * ROWS, (t + 1) * ROWS)
            x, y, z = tile(ex, t), tile(ey, t), tile(ez, t)
            dex = z_next(ex, t) - x
            if t == 0:
                mem = wide(0) * psy[...] + wide(1) * dex
                psy[...] = mem
                dex = dex + mem
            if hx is not None:
                dey = z_next(ey, t) - y
                if t == 0:
                    mem = wide(0) * psx[...] + wide(1) * dey
                    psx[...] = mem
                    dey = dey + mem
                hx[at, :] = tile(hx, t) - COURANT * (y_next(z) - z - dey)
            hy[at, :] = tile(hy, t) - COURANT * (dex - (tile(ez2, t) - z))
            hz[at, :] = tile(hz, t) - COURANT * (tile(ey2, t) - y - (y_next(x) - x))

    def e_plane(p, hy_b, hz_b):
        hx, hy, hz = h.at[0, p], h.at[1, p], h.at[2, p]
        for t in range(tiles):
            at = slice(t * ROWS, (t + 1) * ROWS)
            x, y, z = tile(hx, t), tile(hy, t), tile(hz, t)
            dhy = y - z_prev(hy, t)
            dhx = x - z_prev(hx, t)
            if t == 0:
                mem = wide(2) * psi_e[0, p] + wide(3) * dhy
                psi_e[0, p] = mem
                dhy = dhy + mem
                mem = wide(2) * psi_e[1, p] + wide(3) * dhx
                psi_e[1, p] = mem
                dhx = dhx + mem
            curl = (
                z - y_prev(z) - dhy,
                dhx - (z - tile(hz_b, t)),
                y - tile(hy_b, t) - (x - y_prev(x)),
            )
            inv_eps = coefs[0, p, at, :]
            decay = coefs[1, p, at, :]
            pull = coefs[2, p, at, :]
            hold = coefs[3, p, at, :]
            for c in range(3):
                field = e[c, p, at, :]
                polar = pol[c, p, at, :]
                current = decay * cur[c, p, at, :] + (pull * field - hold * polar)
                cur[c, p, at, :] = current
                pol[c, p, at, :] = polar + current
                e[c, p, at, :] = field + inv_eps * (COURANT * curl[c] - current)

    def to_left(step):
        return pltpu.make_async_remote_copy(
            src_ref=e.at[1:3, 0],
            dst_ref=ahead.at[step],
            send_sem=left_send.at[step],
            recv_sem=left_recv.at[step],
            device_id={"gx": left},
            device_id_type=pl.DeviceIdType.MESH,
        )

    def to_right(step):
        return pltpu.make_async_remote_copy(
            src_ref=e.at[:, planes - 1],
            dst_ref=behind.at[step],
            send_sem=right_send.at[step],
            recv_sem=right_recv.at[step],
            device_id={"gx": right},
            device_id_type=pl.DeviceIdType.MESH,
        )

    firsts = [
        pltpu.make_async_remote_copy(
            src_ref=source,
            dst_ref=target,
            send_sem=first_send.at[index],
            recv_sem=first_recv.at[index],
            device_id={"gx": right},
            device_id_type=pl.DeviceIdType.MESH,
        )
        for index, (source, target) in enumerate(
            [(h.at[1:3, planes - 1], halo), (psi_h.at[1, planes - 1], halo_psi)]
        )
    ]

    def fill_psi(p, carry):
        for source, target in ((psi_h_in, psi_h), (psi_e_in, psi_e)):
            for c in range(2):
                target[c, p] = jnp.zeros((ROWS, cells), jnp.float32)
                for z in range(layers):
                    target[c, p, z : z + 1, :] = source[p, z, c : c + 1, :]
        return carry

    lax.fori_loop(0, planes, fill_psi, 0)
    loads[0].wait()
    loads[1].wait()
    pl.semaphore_wait(barrier, count - 1)
    to_left(0).start()
    to_right(0).start()
    for first in firsts:
        first.start()

    materials = inv_eps_table.shape[0]
    pulls = [drive_table[i] * strength_table[i] for i in range(materials)]
    holds = [drive_table[i] * spring_table[i] for i in range(materials)]
    tables = (
        [inv_eps_table[i] for i in range(materials)],
        [decay_table[i] for i in range(materials)],
        pulls,
        holds,
    )
    loads[2].wait()

    def fill_coefs(p, carry):
        for t in range(tiles):
            at = slice(t * ROWS, (t + 1) * ROWS)
            m = mat[p, at, :]
            same = [m == i for i in range(materials)]
            for index, table in enumerate(tables):
                value = jnp.zeros((ROWS, cells), jnp.float32)
                for i in range(materials):
                    value = jnp.where(same[i], table[i], value)
                coefs[index, p, at, :] = value
        return carry

    lax.fori_loop(0, planes, fill_coefs, 0)

    def h_own(p, ey2, ez2):
        h_plane(
            e.at[0, p], e.at[1, p], e.at[2, p], ey2, ez2,
            h.at[0, p], h.at[1, p], h.at[2, p], psi_h.at[0, p], psi_h.at[1, p],
        )

    def run_step(step, carry):
        def h_inner(p, c):
            h_own(p, e.at[1, p + 1], e.at[2, p + 1])
            return c

        lax.fori_loop(0, planes - 1, h_inner, 0)

        @pl.when(step == 0)
        def _():
            for first in firsts:
                first.wait()
            for load in loads[3:5]:
                load.wait()

        to_left(step).wait()
        h_own(planes - 1, ahead.at[step, 0], ahead.at[step, 1])
        to_right(step).wait()
        h_plane(
            behind.at[step, 0], behind.at[step, 1], behind.at[step, 2],
            e.at[1, 0], e.at[2, 0], None, halo.at[0], halo.at[1], None, halo_psi,
        )
        e_plane(0, halo.at[0], halo.at[1])
        e_plane(planes - 1, h.at[1, planes - 2], h.at[2, planes - 2])

        @pl.when(step < STEPS - 1)
        def _():
            to_left(step + 1).start()
            to_right(step + 1).start()

        def e_inner(p, c):
            e_plane(p, h.at[1, p - 1], h.at[2, p - 1])
            return c

        lax.fori_loop(1, planes - 1, e_inner, 0)
        return carry

    lax.fori_loop(0, STEPS, run_step, 0)

    line[...] = jnp.zeros(line.shape, jnp.float32)
    for c in range(2):
        for p in range(planes):
            line[c * planes + p : c * planes + p + 1, :] = e[c, p, layers : layers + 1, :]
    loads[5].wait()
    gathered[me] = jnp.dot(
        line[...],
        ytab[...],
        precision=lax.Precision.HIGHEST,
        preferred_element_type=jnp.float32,
    )

    def share(k):
        return pltpu.make_async_remote_copy(
            src_ref=gathered.at[me],
            dst_ref=gathered.at[me],
            send_sem=all_send.at[k],
            recv_sem=all_recv.at[me],
            device_id={"gx": lax.rem(me + k, count)},
            device_id_type=pl.DeviceIdType.MESH,
        )

    def start_share(k, carry):
        share(k).start()
        return carry

    lax.fori_loop(1, count, start_share, 0)

    def drain_psi(p, carry):
        for source, target in ((psi_h, psi_h_out), (psi_e, psi_e_out)):
            for c in range(2):
                for z in range(layers):
                    target[p, z, c : c + 1, :] = source[c, p, z : z + 1, :]
        return carry

    lax.fori_loop(0, planes, drain_psi, 0)
    loads[6].wait()

    def end_share(k, carry):
        other = lax.rem(me + k, count)
        pltpu.make_async_remote_copy(
            src_ref=gathered.at[other],
            dst_ref=gathered.at[other],
            send_sem=all_send.at[k],
            recv_sem=all_recv.at[other],
            device_id={"gx": other},
            device_id_type=pl.DeviceIdType.MESH,
        ).wait_recv()
        return carry

    def end_send(k, carry):
        share(k).wait_send()
        return carry

    lax.fori_loop(1, count, end_share, 0)
    lax.fori_loop(1, count, end_send, 0)

    span = KSPAN
    waves = jnp.dot(
        xmat[...],
        gathered[...].reshape(count * line.shape[0], 2 * span),
        precision=lax.Precision.HIGHEST,
        preferred_element_type=jnp.float32,
    )
    scale = 1.0 / math.sqrt(count * planes * cells)
    flats = []
    for c in range(2):
        cosine = waves[2 * c * span : (2 * c + 1) * span]
        sine = waves[(2 * c + 1) * span : (2 * c + 2) * span]
        flats.append(cosine - pltpu.roll(sine, span, 1))
        flats.append(-(pltpu.roll(cosine, span, 1) + sine))
    flat = jnp.concatenate(flats, axis=0)[:, :span] * scale
    pieces = []
    for _ in range(3):
        piece = flat.astype(jnp.bfloat16)
        pieces.append(piece)
        flat = flat - piece.astype(jnp.float32)
    left_side = jnp.concatenate(pieces, axis=1)

    chunk = 512
    total = orders.shape[1]
    index = lax.broadcasted_iota(jnp.int32, (span, chunk), 0) - span // 2
    for start in range(0, total, chunk):
        at = slice(start, start + chunk)
        kx = index == orders[0:1, at]
        ky = jnp.where(index == orders[1:2, at], 1.0, 0.0).astype(jnp.bfloat16)
        picked = jnp.dot(
            left_side,
            jnp.concatenate([ky] * 3, axis=0),
            preferred_element_type=jnp.float32,
        )
        for r in range(4):
            pupil[r : r + 1, at] = jnp.sum(
                jnp.where(kx, picked[r * span : (r + 1) * span], 0.0), axis=0, keepdims=True
            )


def shards(
    e_field,
    h_field,
    polar,
    current,
    psi_h,
    psi_e,
    material,
    inv_eps_table,
    decay_table,
    drive_table,
    strength_table,
    spring_table,
    orders,
):
    count = lax.axis_size("gx")
    planes, depth, cells = material.shape
    layers = psi_h.shape[2]
    f32 = jnp.float32
    rows = -(-2 * planes // ROWS) * ROWS
    prof = jnp.asarray(profile_table(layers))
    ytab = jnp.asarray(wave_table(cells, KSPAN).astype(np.float32))
    xmat = jnp.asarray(x_matrix(count, planes, rows, KSPAN))
    hbm = pl.BlockSpec(memory_space=pltpu.MemorySpace.HBM)
    vmem = pl.BlockSpec(memory_space=pltpu.MemorySpace.VMEM)
    smem = pl.BlockSpec(memory_space=pltpu.MemorySpace.SMEM)
    dma = pltpu.SemaphoreType.DMA
    turned = (planes, layers, 2, cells)
    outs = pl.pallas_call(
        functools.partial(kernel, count, layers),
        out_shape=[jax.ShapeDtypeStruct(e_field.shape, f32)] * 4
        + [jax.ShapeDtypeStruct(turned, f32)] * 2
        + [jax.ShapeDtypeStruct((4, orders.shape[1]), f32)],
        in_specs=[hbm] * 4 + [vmem] * 2 + [hbm] * 3 + [smem] * 5 + [vmem] * 2,
        out_specs=[vmem] * 7,
        scratch_shapes=[
            pltpu.VMEM(material.shape, jnp.int32),
            pltpu.VMEM((4,) + material.shape, f32),
            pltpu.VMEM((2, planes, ROWS, cells), f32),
            pltpu.VMEM((2, planes, ROWS, cells), f32),
            pltpu.VMEM((STEPS, 2, depth, cells), f32),
            pltpu.VMEM((STEPS, 3, depth, cells), f32),
            pltpu.VMEM((2, depth, cells), f32),
            pltpu.VMEM((ROWS, cells), f32),
            pltpu.VMEM(ytab.shape, f32),
            pltpu.VMEM(xmat.shape, f32),
            pltpu.VMEM((rows, cells), f32),
            pltpu.VMEM((count, rows, 2 * KSPAN), f32),
            dma((7,)),
            dma((STEPS,)),
            dma((STEPS,)),
            dma((STEPS,)),
            dma((STEPS,)),
            dma((2,)),
            dma((2,)),
            dma((count,)),
            dma((count,)),
        ],
        compiler_params=pltpu.CompilerParams(
            collective_id=0, has_side_effects=True, vmem_limit_bytes=40 * 1024 * 1024
        ),
    )(
        e_field,
        h_field,
        polar,
        current,
        jnp.transpose(psi_h, (1, 2, 0, 3)),
        jnp.transpose(psi_e, (1, 2, 0, 3)),
        material,
        ytab,
        xmat,
        inv_eps_table,
        decay_table,
        drive_table,
        strength_table,
        spring_table,
        prof,
        orders,
    )
    psi_h_out = jnp.transpose(outs[4], (2, 0, 1, 3))
    psi_e_out = jnp.transpose(outs[5], (2, 0, 1, 3))
    return (outs[0], outs[1], outs[2], outs[3], psi_h_out, psi_e_out, outs[6])


def solution(mesh):
    field = P(None, ("mask", "gx"), None, None)
    in_specs = (field,) * 6 + (P(("mask", "gx"), None, None),) + (P(),) * 6
    out_specs = (field,) * 6 + (P(None, "mask"),)
    return jax.shard_map(shards, mesh=mesh, in_specs=in_specs, out_specs=out_specs, check_vma=False)
```

time: 215 us -> 63.6 us (0.30)
  waiting for transfers between devices: 115 us -> 0 us
  Pallas kernels: 0 us -> 41.2 us
  other arithmetic: 35.5 us -> 0 us
  local copies, waits for them, and re-layouts: 39 us -> 21.1 us
  between operations: 15 us -> 0.67 us
  starting transfers between devices: 6.06 us -> 0 us
    psum x1 -> x0, waiting for transfers between devices: 85 us -> none  [shards(): spectrum = lax.psum(partial_spectrum, 'gx')]
    pallas_call x0 -> x1, Pallas kernels: none -> 41.2 us  [shards(): pl.pallas_call(functools.partial(kernel, count, layers), out_shape=[jax.S...]
    ppermute x8 -> x0, waiting for transfers between devices: 30.1 us -> none  [passed_along(): return lax.ppermute(value, axis, pairs)]
    add x19 -> x0, other arithmetic: 19.5 us -> none  [the longest x3 14.6 us: lookup(): total = total + jnp.where(material == index, table[index], 0.0)]
    gather x1 -> x0, local copies, waits for them, and re-layouts: 14.2 us -> none  [pick_orders(): return jnp.take(flat, index, axis=1)]
    unnamed x85 -> x39, local copies, waits for them, and re-layouts: 10.3 us -> 21.1 us
    slice x57 -> x0, local copies, waits for them, and re-layouts: 8.26 us -> none  [the longest x5 3.22 us: lookup(): total = total + jnp.where(material == index, table[index], 0.0)]
    ppermute x8 -> x0, starting transfers between devices: 6.03 us -> none  [passed_along(): return lax.ppermute(value, axis, pairs)]
  transfers between devices with their start and end apart: 9 -> 0, of which waited for: 8 -> 0; matrix products, arithmetic and copies ran while one was open for 15% -> 0% of each run, Pallas kernels for 0% -> 0%
where the time goes in v1:
time: 63.6 us; the launch traced here: 63 us
  Pallas kernels  41.2 us (65%)
  local copies, waits for them, and re-layouts  21.1 us (33%)
  between operations  0.67 us (1%)
    pallas_call x1, Pallas kernels, shards(): pl.pallas_call(functools.partial(kernel, count, layers), out_shape=[jax.S...  41.2 us
    unnamed x39, local copies, waits for them, and re-layouts  21.1 us

profile of v1, /device:TPU:0, one launch (start us, length us, event | category | flops | bytes accessed | tf_op | source)
XLA Modules:
  0.0 63.0 jit_solution(10327924213248240486)
XLA Ops:
  0.6 0.0 copy-start
  0.6 1.3 %copy-done = f32[3,6,24,768]{3,2,1,0:T(8,128)S(1)} copy-done((f32[3,6,24,768]{3,2,1,0:T(8,128)S(1)}, f32[3,6,24,768]{3,2,1,0:T(8,128)}, u32[]{:S(2)}) %copy-start) | copy-done | bytes 1327128
  2.0 0.0 copy-start.1
  2.0 1.3 %copy-done.1 = f32[3,6,24,768]{3,2,1,0:T(8,128)S(1)} copy-done((f32[3,6,24,768]{3,2,1,0:T(8,128)S(1)}, f32[3,6,24,768]{3,2,1,0:T(8,128)}, u32[]{:S(2)}) %copy-start.1) | copy-done | bytes 1327128
  3.3 0.0 copy-start.2
  3.3 1.3 %copy-done.2 = f32[3,6,24,768]{3,2,1,0:T(8,128)S(1)} copy-done((f32[3,6,24,768]{3,2,1,0:T(8,128)S(1)}, f32[3,6,24,768]{3,2,1,0:T(8,128)}, u32[]{:S(2)}) %copy-start.2) | copy-done | bytes 1327128
  4.6 0.0 copy-start.3
  4.6 1.3 %copy-done.3 = f32[3,6,24,768]{3,2,1,0:T(8,128)S(1)} copy-done((f32[3,6,24,768]{3,2,1,0:T(8,128)S(1)}, f32[3,6,24,768]{3,2,1,0:T(8,128)}, u32[]{:S(2)}) %copy-start.3) | copy-done | bytes 1327128
  5.9 0.0 copy-start.4
  5.9 1.0 %copy-done.4 = s32[6,24,768]{2,1,0:T(8,128)S(1)} copy-done((s32[6,24,768]{2,1,0:T(8,128)S(1)}, s32[6,24,768]{2,1,0:T(8,128)}, u32[]{:S(2)}) %copy-start.4) | copy-done | bytes 442392
  6.9 0.0 copy-start.5
  6.9 1.0 %copy-done.5 = f32[768,128]{1,0:T(8,128)S(1)} copy-done((f32[768,128]{1,0:T(8,128)S(1)}, f32[768,128]{1,0:T(8,128)}, u32[]{:S(2)}) %copy-start.5) | copy-done | bytes 393240
  7.9 0.0 copy-start.6
  7.9 0.9 %copy-done.6 = f32[256,256]{1,0:T(8,128)S(1)} copy-done((f32[256,256]{1,0:T(8,128)S(1)}, f32[256,256]{1,0:T(8,128)}, u32[]{:S(2)}) %copy-start.6) | copy-done | bytes 262168
  8.9 0.0 copy-start.7
  8.9 0.9 %copy-done.7 = f32[2,6,6,768]{3,0,2,1:T(2,128)S(1)} copy-done((f32[2,6,6,768]{3,0,2,1:T(2,128)S(1)}, f32[2,6,6,768]{3,0,2,1:T(2,128)}, u32[]{:S(2)}) %copy-start.7) | copy-done | bytes 221208
  9.8 0.0 copy-start.8
  9.8 0.9 %copy-done.8 = f32[2,6,6,768]{3,0,2,1:T(2,128)S(1)} copy-done((f32[2,6,6,768]{3,0,2,1:T(2,128)S(1)}, f32[2,6,6,768]{3,0,2,1:T(2,128)}, u32[]{:S(2)}) %copy-start.8) | copy-done | bytes 221208
  10.8 0.0 copy-start.9
  10.8 0.8 %copy-done.9 = s32[2,4096]{1,0:T(2,128)S(1)} copy-done((s32[2,4096]{1,0:T(2,128)S(1)}, s32[2,4096]{1,0:T(2,128)}, u32[]{:S(2)}) %copy-start.9) | copy-done | bytes 32792
  11.5 0.0 copy-start.10
  11.5 0.7 %copy-done.10 = f32[4,8,128]{2,1,0:T(8,128)S(1)} copy-done((f32[4,8,128]{2,1,0:T(8,128)S(1)}, f32[4,8,128]{2,1,0:T(8,128)}, u32[]{:S(2)}) %copy-start.10) | copy-done | bytes 16408
  12.2 0.0 copy-start.11
  12.2 0.7 %copy-done.11 = f32[4]{0:T(128)S(1)} copy-done((f32[4]{0:T(128)S(1)}, f32[4]{0:T(128)}, u32[]{:S(2)}) %copy-start.11) | copy-done | bytes 40
  12.9 0.0 copy-start.12
  12.9 0.7 %copy-done.12 = f32[4]{0:T(128)S(1)} copy-done((f32[4]{0:T(128)S(1)}, f32[4]{0:T(128)}, u32[]{:S(2)}) %copy-start.12) | copy-done | bytes 40
  13.6 0.0 copy-start.13
  13.6 0.7 %copy-done.13 = f32[4]{0:T(128)S(1)} copy-done((f32[4]{0:T(128)S(1)}, f32[4]{0:T(128)}, u32[]{:S(2)}) %copy-start.13) | copy-done | bytes 40
  14.2 0.0 copy-start.14
  14.2 0.7 %copy-done.14 = f32[4]{0:T(128)S(1)} copy-done((f32[4]{0:T(128)S(1)}, f32[4]{0:T(128)}, u32[]{:S(2)}) %copy-start.14) | copy-done | bytes 40
  14.9 0.0 copy-start.15
  14.9 0.7 %copy-done.15 = f32[4]{0:T(128)S(1)} copy-done((f32[4]{0:T(128)S(1)}, f32[4]{0:T(128)}, u32[]{:S(2)}) %copy-start.15) | copy-done | bytes 40
  15.5 41.2 %shard_map.207 = (f32[3,6,24,768]{3,2,1,0:T(8,128)S(1)}, f32[3,6,24,768]{3,2,1,0:T(8,128)S(1)}, f32[3,6,24,768]{3,2,1,0:T(8,128)S(1)}, f32[3,6,24,768]{3,2,1,0:T...) custom-call(f32[3,6,24,768]{3,2,1,0:T(8,128)S(1)} %copy-done, ...), custom_call_target="tpu_custom_call" | custom-call | tf_op jit(solution)/shard_map/pallas_call | solution.py:455
  56.7 1.1 %copy.30 = f32[3,6,24,768]{3,2,1,0:T(8,128)} copy(f32[3,6,24,768]{3,2,1,0:T(8,128)S(1)} %get-tuple-element.28) | data formatting | bytes 2654208
  57.8 1.1 %copy.31 = f32[3,6,24,768]{3,2,1,0:T(8,128)} copy(f32[3,6,24,768]{3,2,1,0:T(8,128)S(1)} %get-tuple-element.29) | data formatting | bytes 2654208
  58.8 1.1 %copy.32 = f32[3,6,24,768]{3,2,1,0:T(8,128)} copy(f32[3,6,24,768]{3,2,1,0:T(8,128)S(1)} %get-tuple-element.30) | data formatting | bytes 2654208
  59.9 1.1 %copy.33 = f32[3,6,24,768]{3,2,1,0:T(8,128)} copy(f32[3,6,24,768]{3,2,1,0:T(8,128)S(1)} %get-tuple-element.31) | data formatting | bytes 2654208
  61.0 0.7 %copy.34 = f32[2,6,6,768]{3,0,2,1:T(2,128)} copy(f32[2,6,6,768]{3,0,2,1:T(2,128)S(1)} %bitcast.5) | data formatting | bytes 442368
  61.7 0.7 %copy.35 = f32[2,6,6,768]{3,0,2,1:T(2,128)} copy(f32[2,6,6,768]{3,0,2,1:T(2,128)S(1)} %bitcast.4) | data formatting | bytes 442368
  62.3 0.6 copy.36
Async XLA Ops:
  0.6 1.3 %copy-start = (f32[3,6,24,768]{3,2,1,0:T(8,128)S(1)}, f32[3,6,24,768]{3,2,1,0:T(8,128)}, u32[]{:S(2)}) copy-start(f32[3,6,24,768]{3,2,1,0:T(8,128)} %e_in.1) | copy-start | bytes 3981316
  2.0 1.3 %copy-start.1 = (f32[3,6,24,768]{3,2,1,0:T(8,128)S(1)}, f32[3,6,24,768]{3,2,1,0:T(8,128)}, u32[]{:S(2)}) copy-start(f32[3,6,24,768]{3,2,1,0:T(8,128)} %h_in.1) | copy-start | bytes 3981316
  3.3 1.3 %copy-start.2 = (f32[3,6,24,768]{3,2,1,0:T(8,128)S(1)}, f32[3,6,24,768]{3,2,1,0:T(8,128)}, u32[]{:S(2)}) copy-start(f32[3,6,24,768]{3,2,1,0:T(8,128)} %p_in.1) | copy-start | bytes 3981316
  4.6 1.3 %copy-start.3 = (f32[3,6,24,768]{3,2,1,0:T(8,128)S(1)}, f32[3,6,24,768]{3,2,1,0:T(8,128)}, u32[]{:S(2)}) copy-start(f32[3,6,24,768]{3,2,1,0:T(8,128)} %c_in.1) | copy-start | bytes 3981316
  5.9 1.0 %copy-start.4 = (s32[6,24,768]{2,1,0:T(8,128)S(1)}, s32[6,24,768]{2,1,0:T(8,128)}, u32[]{:S(2)}) copy-start(s32[6,24,768]{2,1,0:T(8,128)} %mat_in.1) | copy-start | bytes 1327108
  6.9 1.0 %copy-start.5 = (f32[768,128]{1,0:T(8,128)S(1)}, f32[768,128]{1,0:T(8,128)}, u32[]{:S(2)}) copy-start(f32[768,128]{1,0:T(8,128)} %constant.7.clone.ytab_in) | copy-start | bytes 1179652
  7.9 0.9 %copy-start.6 = (f32[256,256]{1,0:T(8,128)S(1)}, f32[256,256]{1,0:T(8,128)}, u32[]{:S(2)}) copy-start(f32[256,256]{1,0:T(8,128)} %constant.8.clone.xmat_in) | copy-start | bytes 786436
  8.9 0.9 %copy-start.7 = (f32[2,6,6,768]{3,0,2,1:T(2,128)S(1)}, f32[2,6,6,768]{3,0,2,1:T(2,128)}, u32[]{:S(2)}) copy-start(f32[2,6,6,768]{3,0,2,1:T(2,128)} %param.20) | copy-start | bytes 663556
  9.8 0.9 %copy-start.8 = (f32[2,6,6,768]{3,0,2,1:T(2,128)S(1)}, f32[2,6,6,768]{3,0,2,1:T(2,128)}, u32[]{:S(2)}) copy-start(f32[2,6,6,768]{3,0,2,1:T(2,128)} %param.21) | copy-start | bytes 663556
  10.8 0.8 %copy-start.9 = (s32[2,4096]{1,0:T(2,128)S(1)}, s32[2,4096]{1,0:T(2,128)}, u32[]{:S(2)}) copy-start(s32[2,4096]{1,0:T(2,128)} %orders.1) | copy-start | bytes 98308
  11.5 0.7 %copy-start.10 = (f32[4,8,128]{2,1,0:T(8,128)S(1)}, f32[4,8,128]{2,1,0:T(8,128)}, u32[]{:S(2)}) copy-start(f32[4,8,128]{2,1,0:T(8,128)} %constant.6.clone.prof) | copy-start | bytes 49156
  12.2 0.7 %copy-start.11 = (f32[4]{0:T(128)S(1)}, f32[4]{0:T(128)}, u32[]{:S(2)}) copy-start(f32[4]{0:T(128)} %inv_eps_table.1) | copy-start | bytes 52
  12.9 0.7 %copy-start.12 = (f32[4]{0:T(128)S(1)}, f32[4]{0:T(128)}, u32[]{:S(2)}) copy-start(f32[4]{0:T(128)} %decay_table.1) | copy-start | bytes 52
  13.6 0.7 %copy-start.13 = (f32[4]{0:T(128)S(1)}, f32[4]{0:T(128)}, u32[]{:S(2)}) copy-start(f32[4]{0:T(128)} %drive_table.1) | copy-start | bytes 52
  14.2 0.7 %copy-start.14 = (f32[4]{0:T(128)S(1)}, f32[4]{0:T(128)}, u32[]{:S(2)}) copy-start(f32[4]{0:T(128)} %strength_table.1) | copy-start | bytes 52
  14.9 0.7 %copy-start.15 = (f32[4]{0:T(128)S(1)}, f32[4]{0:T(128)}, u32[]{:S(2)}) copy-start(f32[4]{0:T(128)} %spring_table.1) | copy-start | bytes 52

commit v2 on v1

v2 whole, which is shorter than its diff:
```python
import functools
import math

import jax
import jax.numpy as jnp
import numpy as np
from jax import lax
from jax.experimental import pallas as pl
from jax.experimental.pallas import tpu as pltpu
from jax.sharding import PartitionSpec as P

KSPAN = 64
STEPS = 4
COURANT = 0.5
SIGMA_MAX = 0.8
PML_ALPHA = 0.05
ROWS = 8
LANES = 128


def profile_values(layers):
    out = []
    for offset in (0.5, 0.0):
        depth = (layers - np.arange(layers, dtype=np.float64) - offset) / layers
        sigma = SIGMA_MAX * depth**3
        decay = np.exp(-(sigma + PML_ALPHA))
        gain = sigma / (sigma + PML_ALPHA) * (decay - 1.0)
        out += [decay, gain]
    return out


def wave_table(cells, span):
    rows = np.arange(cells, dtype=np.int64)
    waves = np.arange(span, dtype=np.int64) - span // 2
    phase = (rows[:, None] * waves[None, :] % cells) * (2.0 * math.pi / cells)
    return np.concatenate([np.cos(phase), np.sin(phase)], axis=1)


def x_matrix(count, planes, rows, span):
    waves = wave_table(count * planes, span).T.reshape(2 * span, count, planes)
    out = np.zeros((2, 2 * span, count, rows))
    for comp in range(2):
        out[comp, :, :, comp * planes : (comp + 1) * planes] = waves
    return out.reshape(4 * span, count * rows).astype(np.float32)


def step_kernel(
    count,
    layers,
    e_in,
    h_in,
    p_in,
    c_in,
    psi_h_in,
    psi_e_in,
    mat_in,
    ytab_in,
    inv_eps_table,
    decay_table,
    drive_table,
    strength_table,
    spring_table,
    e_out,
    h_out,
    p_out,
    c_out,
    psi_h_out,
    psi_e_out,
    gathered_out,
    e,
    h,
    pol,
    cur,
    raw_h,
    raw_e,
    mat,
    prof,
    coefs,
    psi_h,
    psi_e,
    ahead,
    behind,
    ytab,
    line,
    gathered,
    load_sem,
    store_sem,
    left_send,
    left_recv,
    right_send,
    right_recv,
    all_send,
    all_recv,
):
    planes, depth, cells = mat.shape
    tiles = depth // ROWS
    last = planes - 1
    me = lax.axis_index("gx")
    right, left = lax.rem(me + 1, count), lax.rem(me + count - 1, count)

    loads = [
        pltpu.make_async_copy(source, target, load_sem.at[index])
        for index, (source, target) in enumerate(
            [
                (e_in, e),
                (h_in, h),
                (psi_h_in, raw_h),
                (mat_in, mat),
                (c_in, cur),
                (p_in, pol),
                (psi_e_in, raw_e),
                (ytab_in, ytab),
            ]
        )
    ]
    for load in loads:
        load.start()
    stores = [
        pltpu.make_async_copy(source, target, store_sem.at[index])
        for index, (source, target) in enumerate(
            [
                (h, h_out),
                (e, e_out),
                (cur, c_out),
                (pol, p_out),
                (raw_h, psi_h_out),
                (raw_e, psi_e_out),
                (gathered, gathered_out),
            ]
        )
    ]

    barrier = pltpu.get_barrier_semaphore()

    def greet(k, carry):
        pl.semaphore_signal(
            barrier,
            inc=1,
            device_id={"gx": lax.rem(me + k, count)},
            device_id_type=pl.DeviceIdType.MESH,
        )
        return carry

    lax.fori_loop(1, count, greet, 0)

    level = lax.broadcasted_iota(jnp.int32, (ROWS, LANES), 0)
    for index, values in enumerate(profile_values(layers)):
        total = jnp.zeros((ROWS, LANES), jnp.float32)
        for z in range(layers):
            total = jnp.where(level == z, float(values[z]), total)
        prof[index] = total

    row = lax.broadcasted_iota(jnp.int32, (ROWS, cells), 0)
    first_row = row == 0
    last_row = row == ROWS - 1

    def wide(index):
        return jnp.concatenate([prof[index]] * (cells // LANES), axis=1)

    def rows_of(t):
        return slice(t * ROWS, (t + 1) * ROWS)

    def tile(ref, t):
        return ref[rows_of(t), :]

    def z_next(ref, t):
        moved = pltpu.roll(tile(ref, t), ROWS - 1, 0)
        if t == tiles - 1:
            return jnp.where(last_row, 0.0, moved)
        return jnp.where(last_row, ref[(t + 1) * ROWS : (t + 1) * ROWS + 1, :], moved)

    def z_prev(ref, t):
        moved = pltpu.roll(tile(ref, t), 1, 0)
        if t == 0:
            return jnp.where(first_row, 0.0, moved)
        return jnp.where(first_row, ref[t * ROWS - 1 : t * ROWS, :], moved)

    def y_next(value):
        return pltpu.roll(value, cells - 1, 1)

    def y_prev(value):
        return pltpu.roll(value, 1, 1)

    def h_tile(p, t, whole):
        at = rows_of(t)
        ex, ey = e.at[0, p], e.at[1, p]
        x, y, z = tile(ex, t), tile(ey, t), e[2, p, at, :]
        dex = z_next(ex, t) - x
        dey = z_next(ey, t) - y
        if t == 0:
            mem = wide(0) * psi_h[1, p] + wide(1) * dex
            psi_h[1, p] = mem
            dex = dex + mem
            mem = wide(0) * psi_h[0, p] + wide(1) * dey
            psi_h[0, p] = mem
            dey = dey + mem
        h[0, p, at, :] = h[0, p, at, :] - COURANT * (y_next(z) - z - dey)
        part_y = dex + z
        part_z = x - y - y_next(x)
        if whole:
            part_y = part_y - e[2, p + 1, at, :]
            part_z = part_z + e[1, p + 1, at, :]
        h[1, p, at, :] = h[1, p, at, :] - COURANT * part_y
        h[2, p, at, :] = h[2, p, at, :] - COURANT * part_z

    def e_tile(p, t, hy_b, hz_b):
        at = rows_of(t)
        hx, hy = h.at[0, p], h.at[1, p]
        x, y, z = tile(hx, t), tile(hy, t), h[2, p, at, :]
        dhy = y - z_prev(hy, t)
        dhx = x - z_prev(hx, t)
        if t == 0:
            mem = wide(2) * psi_e[0, p] + wide(3) * dhy
            psi_e[0, p] = mem
            dhy = dhy + mem
            mem = wide(2) * psi_e[1, p] + wide(3) * dhx
            psi_e[1, p] = mem
            dhx = dhx + mem
        curl = (
            z - y_prev(z) - dhy,
            dhx - (z - hz_b),
            y - hy_b - (x - y_prev(x)),
        )
        inv_eps = coefs[0, p, at, :]
        decay = coefs[1, p, at, :]
        pull = coefs[2, p, at, :]
        hold = coefs[3, p, at, :]
        for c in range(3):
            field = e[c, p, at, :]
            polar = pol[c, p, at, :]
            current = decay * cur[c, p, at, :] + (pull * field - hold * polar)
            cur[c, p, at, :] = current
            pol[c, p, at, :] = polar + current
            e[c, p, at, :] = field + inv_eps * (COURANT * curl[c] - current)

    def e_own(p, t):
        e_tile(p, t, h[1, p - 1, rows_of(t), :], h[2, p - 1, rows_of(t), :])

    def to_left(step, t):
        return pltpu.make_async_remote_copy(
            src_ref=e.at[1:3, 0, rows_of(t)],
            dst_ref=ahead.at[step, :, rows_of(t)],
            send_sem=left_send.at[step, t],
            recv_sem=left_recv.at[step, t],
            device_id={"gx": left},
            device_id_type=pl.DeviceIdType.MESH,
        )

    def to_right(step, t):
        return pltpu.make_async_remote_copy(
            src_ref=h.at[1:3, last, rows_of(t)],
            dst_ref=behind.at[step, :, rows_of(t)],
            send_sem=right_send.at[step, t],
            recv_sem=right_recv.at[step, t],
            device_id={"gx": right},
            device_id_type=pl.DeviceIdType.MESH,
        )

    def fill_psi(source, target):
        def fill(p, carry):
            for c in range(2):
                target[c, p] = jnp.zeros((ROWS, cells), jnp.float32)
                for z in range(layers):
                    target[c, p, z : z + 1, :] = source[p, z, c : c + 1, :]
            return carry

        lax.fori_loop(0, planes, fill, 0)

    def drain_psi(source, target):
        def drain(p, carry):
            for c in range(2):
                for z in range(layers):
                    target[p, z, c : c + 1, :] = source[c, p, z : z + 1, :]
            return carry

        lax.fori_loop(0, planes, drain, 0)

    for load in loads[:3]:
        load.wait()
    fill_psi(raw_h, psi_h)
    h_tile(last, 0, False)
    pl.semaphore_wait(barrier, count - 1)
    for t in range(tiles):
        to_left(0, t).start()
        if t > 0:
            h_tile(last, t, False)
        to_right(0, t).start()

    materials = inv_eps_table.shape[0]
    tables = (
        [inv_eps_table[i] for i in range(materials)],
        [decay_table[i] for i in range(materials)],
        [drive_table[i] * strength_table[i] for i in range(materials)],
        [drive_table[i] * spring_table[i] for i in range(materials)],
    )
    loads[3].wait()

    def fill_coefs(p, carry):
        for t in range(tiles):
            m = mat[p, rows_of(t), :]
            same = [m == i for i in range(materials)]
            for index, table in enumerate(tables):
                value = jnp.zeros((ROWS, cells), jnp.float32)
                for i in range(materials):
                    value = jnp.where(same[i], table[i], value)
                coefs[index, p, rows_of(t), :] = value
        return carry

    lax.fori_loop(0, planes, fill_coefs, 0)
    for load in loads[4:]:
        load.wait()
    fill_psi(raw_e, psi_e)

    def run_step(step, carry):
        def h_inner(p, c):
            for t in range(tiles):
                h_tile(p, t, True)
            return c

        lax.fori_loop(0, last, h_inner, 0)
        more = step < STEPS - 1

        def next_right(t):
            h_tile(last, t, False)
            to_right(step + 1, t).start()

        for t in range(tiles):
            at = rows_of(t)
            to_left(step, t).wait()
            to_right(step, t).wait()
            h[1, last, at, :] = h[1, last, at, :] + COURANT * ahead[step, 1, at, :]
            h[2, last, at, :] = h[2, last, at, :] - COURANT * ahead[step, 0, at, :]
            hy_b = behind[step, 0, at, :] + COURANT * e[2, 0, at, :]
            hz_b = behind[step, 1, at, :] - COURANT * e[1, 0, at, :]
            e_tile(0, t, hy_b, hz_b)

            @pl.when(more)
            def _():
                to_left(step + 1, t).start()

            e_own(last, t)

            @pl.when(more)
            def _():
                if t > 0:
                    next_right(t - 1)
                if t == tiles - 1:
                    next_right(t)

        @pl.when(jnp.logical_not(more))
        def _():
            stores[0].start()

        def e_inner(p, c):
            for t in range(tiles):
                e_own(p, t)
            return c

        lax.fori_loop(1, last, e_inner, 0)
        return carry

    lax.fori_loop(0, STEPS, run_step, 0)

    line[...] = jnp.zeros(line.shape, jnp.float32)
    for c in range(2):
        for p in range(planes):
            line[c * planes + p : c * planes + p + 1, :] = e[c, p, layers : layers + 1, :]
    gathered[me] = jnp.dot(
        line[...],
        ytab[...],
        precision=lax.Precision.HIGHEST,
        preferred_element_type=jnp.float32,
    )

    def share(k):
        return pltpu.make_async_remote_copy(
            src_ref=gathered.at[me],
            dst_ref=gathered.at[me],
            send_sem=all_send.at[k],
            recv_sem=all_recv.at[me],
            device_id={"gx": lax.rem(me + k, count)},
            device_id_type=pl.DeviceIdType.MESH,
        )

    def start_share(k, carry):
        share(k).start()
        return carry

    lax.fori_loop(1, count, start_share, 0)
    for store in stores[1:4]:
        store.start()
    drain_psi(psi_h, raw_h)
    stores[4].start()
    drain_psi(psi_e, raw_e)
    stores[5].start()

    def end_share(k, carry):
        other = lax.rem(me + k, count)
        pltpu.make_async_remote_copy(
            src_ref=gathered.at[other],
            dst_ref=gathered.at[other],
            send_sem=all_send.at[k],
            recv_sem=all_recv.at[other],
            device_id={"gx": other},
            device_id_type=pl.DeviceIdType.MESH,
        ).wait_recv()
        return carry

    def end_send(k, carry):
        share(k).wait_send()
        return carry

    lax.fori_loop(1, count, end_share, 0)
    lax.fori_loop(1, count, end_send, 0)
    stores[6].start()
    for store in stores:
        store.wait()


def result_kernel(norm, *refs):
    ins, refs = refs[:6], refs[6:]
    (gathered_in, xmat_in, orders), refs = refs[:3], refs[3:]
    outs, pupil, refs = refs[:6], refs[6], refs[7:]
    held, (gathered, xmat, in_sem, out_sem, table_sem) = refs[:6], refs[6:]

    tables = [
        pltpu.make_async_copy(gathered_in, gathered, table_sem.at[0]),
        pltpu.make_async_copy(xmat_in, xmat, table_sem.at[1]),
    ]
    for table in tables:
        table.start()
    loads, stores = [], []
    for index in range(6):
        for c in range(held[index].shape[0]):
            sem = len(loads)
            loads.append(
                pltpu.make_async_copy(ins[index].at[c], held[index].at[c], in_sem.at[sem])
            )
            stores.append(
                pltpu.make_async_copy(held[index].at[c], outs[index].at[c], out_sem.at[sem])
            )
    for load in loads:
        load.start()
    for table in tables:
        table.wait()

    span = KSPAN
    waves = jnp.dot(
        xmat[...],
        gathered[...].reshape(gathered.shape[0] * gathered.shape[1], 2 * span),
        precision=lax.Precision.HIGHEST,
        preferred_element_type=jnp.float32,
    )
    for load, store in zip(loads, stores):
        load.wait()
        store.start()
    flats = []
    for c in range(2):
        cosine = waves[2 * c * span : (2 * c + 1) * span]
        sine = waves[(2 * c + 1) * span : (2 * c + 2) * span]
        flats.append(cosine - pltpu.roll(sine, span, 1))
        flats.append(-(pltpu.roll(cosine, span, 1) + sine))
    flat = jnp.concatenate(flats, axis=0)[:, :span] * norm
    pieces = []
    for _ in range(3):
        piece = flat.astype(jnp.bfloat16)
        pieces.append(piece)
        flat = flat - piece.astype(jnp.float32)
    left_side = jnp.concatenate(pieces, axis=1)

    chunk = 512
    total = orders.shape[1]
    index = lax.broadcasted_iota(jnp.int32, (span, chunk), 0) - span // 2
    for start in range(0, total, chunk):
        at = slice(start, start + chunk)
        kx = index == orders[0:1, at]
        ky = jnp.where(index == orders[1:2, at], 1.0, 0.0).astype(jnp.bfloat16)
        picked = jnp.dot(
            left_side,
            jnp.concatenate([ky] * 3, axis=0),
            preferred_element_type=jnp.float32,
        )
        for r in range(4):
            pupil[r : r + 1, at] = jnp.sum(
                jnp.where(kx, picked[r * span : (r + 1) * span], 0.0), axis=0, keepdims=True
            )
    for store in stores:
        store.wait()


def shards(
    e_field,
    h_field,
    polar,
    current,
    psi_h,
    psi_e,
    material,
    inv_eps_table,
    decay_table,
    drive_table,
    strength_table,
    spring_table,
    orders,
):
    count = lax.axis_size("gx")
    planes, depth, cells = material.shape
    layers = psi_h.shape[2]
    f32 = jnp.float32
    rows = -(-2 * planes // ROWS) * ROWS
    ytab = jnp.asarray(wave_table(cells, KSPAN).astype(np.float32))
    xmat = jnp.asarray(x_matrix(count, planes, rows, KSPAN))
    hbm = pl.BlockSpec(memory_space=pltpu.MemorySpace.HBM)
    vmem = pl.BlockSpec(memory_space=pltpu.MemorySpace.VMEM)
    smem = pl.BlockSpec(memory_space=pltpu.MemorySpace.SMEM)
    dma = pltpu.SemaphoreType.DMA
    limit = 56 * 1024 * 1024
    turned = (planes, layers, 2, cells)
    field = e_field.shape
    shape = jax.ShapeDtypeStruct
    state = [shape(field, f32)] * 4 + [shape(turned, f32)] * 2
    lines = (count, rows, 2 * KSPAN)
    edges = (STEPS, depth // ROWS)
    outs = pl.pallas_call(
        functools.partial(step_kernel, count, layers),
        out_shape=state + [shape(lines, f32)],
        in_specs=[hbm] * 8 + [smem] * 5,
        out_specs=[hbm] * 7,
        scratch_shapes=[pltpu.VMEM(field, f32)] * 4
        + [pltpu.VMEM(turned, f32)] * 2
        + [
            pltpu.VMEM(material.shape, jnp.int32),
            pltpu.VMEM((4, ROWS, LANES), f32),
            pltpu.VMEM((4,) + material.shape, f32),
            pltpu.VMEM((2, planes, ROWS, cells), f32),
            pltpu.VMEM((2, planes, ROWS, cells), f32),
            pltpu.VMEM((STEPS, 2, depth, cells), f32),
            pltpu.VMEM((STEPS, 2, depth, cells), f32),
            pltpu.VMEM(ytab.shape, f32),
            pltpu.VMEM((rows, cells), f32),
            pltpu.VMEM(lines, f32),
            dma((8,)),
            dma((7,)),
            dma(edges),
            dma(edges),
            dma(edges),
            dma(edges),
            dma((count,)),
            dma((count,)),
        ],
        compiler_params=pltpu.CompilerParams(
            collective_id=0, has_side_effects=True, vmem_limit_bytes=limit
        ),
    )(
        e_field,
        h_field,
        polar,
        current,
        jnp.transpose(psi_h, (1, 2, 0, 3)),
        jnp.transpose(psi_e, (1, 2, 0, 3)),
        material,
        ytab,
        inv_eps_table,
        decay_table,
        drive_table,
        strength_table,
        spring_table,
    )
    copies = 4 * field[0] + 2 * planes
    results = pl.pallas_call(
        functools.partial(result_kernel, 1.0 / math.sqrt(count * planes * cells)),
        out_shape=state + [shape((4, orders.shape[1]), f32)],
        in_specs=[hbm] * 8 + [vmem],
        out_specs=[hbm] * 6 + [vmem],
        scratch_shapes=[pltpu.VMEM(field, f32)] * 4
        + [pltpu.VMEM(turned, f32)] * 2
        + [
            pltpu.VMEM(lines, f32),
            pltpu.VMEM(xmat.shape, f32),
            dma((copies,)),
            dma((copies,)),
            dma((2,)),
        ],
        compiler_params=pltpu.CompilerParams(vmem_limit_bytes=limit),
    )(*outs, xmat, orders)
    psi_h_out = jnp.transpose(results[4], (2, 0, 1, 3))
    psi_e_out = jnp.transpose(results[5], (2, 0, 1, 3))
    return (*results[:4], psi_h_out, psi_e_out, results[6])


def solution(mesh):
    field = P(None, ("mask", "gx"), None, None)
    in_specs = (field,) * 6 + (P(("mask", "gx"), None, None),) + (P(),) * 6
    out_specs = (field,) * 6 + (P(None, "mask"),)
    return jax.shard_map(shards, mesh=mesh, in_specs=in_specs, out_specs=out_specs, check_vma=False)
```

time: 63.6 us -> 39 us (0.61)
  local copies, waits for them, and re-layouts: 21.1 us -> 0 us
  Pallas kernels: 41.2 us -> 38.1 us
    unnamed x39 -> x0, local copies, waits for them, and re-layouts: 21.1 us -> none
    pallas_call x1 -> x2, Pallas kernels: 41.2 us -> 38.1 us  [the longest x1 30.6 us: shards(): pl.pallas_call(functools.partial(step_kernel, count, layers), out_shape=s...]
where the time goes in v2:
time: 39 us; the launch traced here: 38.8 us
  Pallas kernels  38.1 us (98%)
  between operations  0.65 us (2%)
    pallas_call x1, Pallas kernels, shards(): pl.pallas_call(functools.partial(step_kernel, count, layers), out_shape=s...  30.6 us
    pallas_call x1, Pallas kernels, shards(): pl.pallas_call(functools.partial(result_kernel, 1.0 / math.sqrt(count * p...  7.54 us

profile of v2, /device:TPU:0, one launch (start us, length us, event | category | flops | bytes accessed | tf_op | source)
XLA Modules:
  0.0 38.8 jit_solution(16992639654932005382)
XLA Ops:
  0.6 30.6 %shard_map.198 = (f32[3,6,24,768]{3,2,1,0:T(8,128)}, f32[3,6,24,768]{3,2,1,0:T(8,128)}, f32[3,6,24,768]{3,2,1,0:T(8,128)}, f32[3,6,24,768]{3,2,1,0:T(8,128)}, f3...) custom-call(f32[3,6,24,768]{3,2,1,0:T(8,128)} %e_in.1, f32[3,6,24,768]{3,2,1,0:T(8,128)} %h_in.1, ...), custom_call_target="tpu_custom_call" | custom-call | tf_op jit(solution)/shard_map/pallas_call | solution.py:524
  31.2 7.5 %shard_map.199 = (f32[3,6,24,768]{3,2,1,0:T(8,128)}, f32[3,6,24,768]{3,2,1,0:T(8,128)}, f32[3,6,24,768]{3,2,1,0:T(8,128)}, f32[3,6,24,768]{3,2,1,0:T(8,128)}, f3...) custom-call(f32[3,6,24,768]{3,2,1,0:T(8,128)} %get-tuple-element.21.refs_0_, ...), custom_call_target="tpu_custom_call" | custom-call | tf_op jit(solution)/shard_map/pallas_call | solution.py:570

commit v3 on v2

--- a/solution.py
+++ b/solution.py
@@ -55,18 +55,20 @@
     psi_e_in,
     mat_in,
     ytab_in,
+    xmat_in,
     inv_eps_table,
     decay_table,
     drive_table,
     strength_table,
     spring_table,
+    orders,
     e_out,
     h_out,
     p_out,
     c_out,
     psi_h_out,
     psi_e_out,
-    gathered_out,
+    pupil_out,
     e,
     h,
     pol,
@@ -83,6 +85,8 @@
     ytab,
     line,
     gathered,
+    xmat,
+    pupil,
     load_sem,
     store_sem,
     left_send,
@@ -110,6 +114,7 @@
                 (p_in, pol),
                 (psi_e_in, raw_e),
                 (ytab_in, ytab),
+                (xmat_in, xmat),
             ]
         )
     ]
@@ -125,7 +130,7 @@
                 (pol, p_out),
                 (raw_h, psi_h_out),
                 (raw_e, psi_e_out),
-                (gathered, gathered_out),
+                (pupil, pupil_out),
             ]
         )
     ]
@@ -311,6 +316,33 @@
         load.wait()
     fill_psi(raw_e, psi_e)
 
+    def share(k):
+        return pltpu.make_async_remote_copy(
+            src_ref=gathered.at[me],
+            dst_ref=gathered.at[me],
+            send_sem=all_send.at[k],
+            recv_sem=all_recv.at[me],
+            device_id={"gx": lax.rem(me + k, count)},
+            device_id_type=pl.DeviceIdType.MESH,
+        )
+
+    def start_share(k, carry):
+        share(k).start()
+        return carry
+
+    def transform():
+        line[...] = jnp.zeros(line.shape, jnp.float32)
+        for c in range(2):
+            for p in range(planes):
+                line[c * planes + p : c * planes + p + 1, :] = e[c, p, layers : layers + 1, :]
+        gathered[me] = jnp.dot(
+            line[...],
+            ytab[...],
+            precision=lax.Precision.HIGHEST,
+            preferred_element_type=jnp.float32,
+        )
+        lax.fori_loop(1, count, start_share, 0)
+
     def run_step(step, carry):
         def h_inner(p, c):
             for t in range(tiles):
@@ -324,7 +356,18 @@
             h_tile(last, t, False)
             to_right(step + 1, t).start()
 
+        def e_first(p, c):
+            e_own(p, 0)
+            return c
+
         for t in range(tiles):
+            if t == 1:
+                lax.fori_loop(1, last, e_first, 0)
+
+                @pl.when(jnp.logical_not(more))
+                def _():
+                    transform()
+
             at = rows_of(t)
             to_left(step, t).wait()
             to_right(step, t).wait()
@@ -352,7 +395,7 @@
             stores[0].start()
 
         def e_inner(p, c):
-            for t in range(tiles):
+            for t in range(1, tiles):
                 e_own(p, t)
             return c
 
@@ -361,32 +404,6 @@
 
     lax.fori_loop(0, STEPS, run_step, 0)
 
-    line[...] = jnp.zeros(line.shape, jnp.float32)
-    for c in range(2):
-        for p in range(planes):
-            line[c * planes + p : c * planes + p + 1, :] = e[c, p, layers : layers + 1, :]
-    gathered[me] = jnp.dot(
-        line[...],
-        ytab[...],
-        precision=lax.Precision.HIGHEST,
-        preferred_element_type=jnp.float32,
-    )
-
-    def share(k):
-        return pltpu.make_async_remote_copy(
-            src_ref=gathered.at[me],
-            dst_ref=gathered.at[me],
-            send_sem=all_send.at[k],
-            recv_sem=all_recv.at[me],
-            device_id={"gx": lax.rem(me + k, count)},
-            device_id_type=pl.DeviceIdType.MESH,
-        )
-
-    def start_share(k, carry):
-        share(k).start()
-        return carry
-
-    lax.fori_loop(1, count, start_share, 0)
     for store in stores[1:4]:
         store.start()
     drain_psi(psi_h, raw_h)
@@ -412,37 +429,6 @@
 
     lax.fori_loop(1, count, end_share, 0)
     lax.fori_loop(1, count, end_send, 0)
-    stores[6].start()
-    for store in stores:
-        store.wait()
-
-
-def result_kernel(norm, *refs):
-    ins, refs = refs[:6], refs[6:]
-    (gathered_in, xmat_in, orders), refs = refs[:3], refs[3:]
-    outs, pupil, refs = refs[:6], refs[6], refs[7:]
-    held, (gathered, xmat, in_sem, out_sem, table_sem) = refs[:6], refs[6:]
-
-    tables = [
-        pltpu.make_async_copy(gathered_in, gathered, table_sem.at[0]),
-        pltpu.make_async_copy(xmat_in, xmat, table_sem.at[1]),
-    ]
-    for table in tables:
-        table.start()
-    loads, stores = [], []
-    for index in range(6):
-        for c in range(held[index].shape[0]):
-            sem = len(loads)
-            loads.append(
-                pltpu.make_async_copy(ins[index].at[c], held[index].at[c], in_sem.at[sem])
-            )
-            stores.append(
-                pltpu.make_async_copy(held[index].at[c], outs[index].at[c], out_sem.at[sem])
-            )
-    for load in loads:
-        load.start()
-    for table in tables:
-        table.wait()
 
     span = KSPAN
     waves = jnp.dot(
@@ -451,16 +437,13 @@
         precision=lax.Precision.HIGHEST,
         preferred_element_type=jnp.float32,
     )
-    for load, store in zip(loads, stores):
-        load.wait()
-        store.start()
     flats = []
     for c in range(2):
         cosine = waves[2 * c * span : (2 * c + 1) * span]
         sine = waves[(2 * c + 1) * span : (2 * c + 2) * span]
         flats.append(cosine - pltpu.roll(sine, span, 1))
         flats.append(-(pltpu.roll(cosine, span, 1) + sine))
-    flat = jnp.concatenate(flats, axis=0)[:, :span] * norm
+    flat = jnp.concatenate(flats, axis=0)[:, :span] * (1.0 / math.sqrt(count * planes * cells))
     pieces = []
     for _ in range(3):
         piece = flat.astype(jnp.bfloat16)
@@ -484,6 +467,29 @@
             pupil[r : r + 1, at] = jnp.sum(
                 jnp.where(kx, picked[r * span : (r + 1) * span], 0.0), axis=0, keepdims=True
             )
+    stores[6].start()
+    for store in stores:
+        store.wait()
+
+
+def result_kernel(*refs):
+    ins, outs, held, (in_sem, out_sem) = refs[:7], refs[7:14], refs[14:21], refs[21:]
+    loads, stores = [], []
+    for source, target, buffer in zip(ins, outs, held):
+        pieces = [slice(None)] if len(buffer.shape) == 2 else range(buffer.shape[0])
+        for piece in pieces:
+            sem = len(loads)
+            loads.append(
+                pltpu.make_async_copy(source.at[piece], buffer.at[piece], in_sem.at[sem])
+            )
+            stores.append(
+                pltpu.make_async_copy(buffer.at[piece], target.at[piece], out_sem.at[sem])
+            )
+    for load in loads:
+        load.start()
+    for load, store in zip(loads, stores):
+        load.wait()
+        store.start()
     for store in stores:
         store.wait()
 
@@ -518,13 +524,14 @@
     turned = (planes, layers, 2, cells)
     field = e_field.shape
     shape = jax.ShapeDtypeStruct
-    state = [shape(field, f32)] * 4 + [shape(turned, f32)] * 2
+    found = (4, orders.shape[1])
+    state = [shape(field, f32)] * 4 + [shape(turned, f32)] * 2 + [shape(found, f32)]
     lines = (count, rows, 2 * KSPAN)
     edges = (STEPS, depth // ROWS)
     outs = pl.pallas_call(
         functools.partial(step_kernel, count, layers),
-        out_shape=state + [shape(lines, f32)],
-        in_specs=[hbm] * 8 + [smem] * 5,
+        out_shape=state,
+        in_specs=[hbm] * 9 + [smem] * 5 + [vmem],
         out_specs=[hbm] * 7,
         scratch_shapes=[pltpu.VMEM(field, f32)] * 4
         + [pltpu.VMEM(turned, f32)] * 2
@@ -539,7 +546,9 @@
             pltpu.VMEM(ytab.shape, f32),
             pltpu.VMEM((rows, cells), f32),
             pltpu.VMEM(lines, f32),
-            dma((8,)),
+            pltpu.VMEM(xmat.shape, f32),
+            pltpu.VMEM(found, f32),
+            dma((9,)),
             dma((7,)),
             dma(edges),
             dma(edges),
@@ -560,29 +569,25 @@
         jnp.transpose(psi_e, (1, 2, 0, 3)),
         material,
         ytab,
+        xmat,
         inv_eps_table,
         decay_table,
         drive_table,
         strength_table,
         spring_table,
+        orders,
     )
-    copies = 4 * field[0] + 2 * planes
+    copies = 4 * field[0] + 2 * planes + 1
     results = pl.pallas_call(
-        functools.partial(result_kernel, 1.0 / math.sqrt(count * planes * cells)),
-        out_shape=state + [shape((4, orders.shape[1]), f32)],
-        in_specs=[hbm] * 8 + [vmem],
-        out_specs=[hbm] * 6 + [vmem],
+        result_kernel,
+        out_shape=state,
+        in_specs=[hbm] * 7,
+        out_specs=[hbm] * 7,
         scratch_shapes=[pltpu.VMEM(field, f32)] * 4
         + [pltpu.VMEM(turned, f32)] * 2
-        + [
-            pltpu.VMEM(lines, f32),
-            pltpu.VMEM(xmat.shape, f32),
-            dma((copies,)),
-            dma((copies,)),
-            dma((2,)),
-        ],
+        + [pltpu.VMEM(found, f32), dma((copies,)), dma((copies,))],
         compiler_params=pltpu.CompilerParams(vmem_limit_bytes=limit),
-    )(*outs, xmat, orders)
+    )(*outs)
     psi_h_out = jnp.transpose(results[4], (2, 0, 1, 3))
     psi_e_out = jnp.transpose(results[5], (2, 0, 1, 3))
     return (*results[:4], psi_h_out, psi_e_out, results[6])

time: 39 us -> 37.1 us (0.951)
  Pallas kernels: 38.1 us -> 36.3 us
    pallas_call x1, Pallas kernels: 7.54 us -> 5.23 us  [shards(): pl.pallas_call(result_kernel, out_shape=state, in_specs=[hbm] * 7, out_sp...]
    pallas_call x1, Pallas kernels: 30.6 us -> 31.1 us  [shards(): pl.pallas_call(functools.partial(step_kernel, count, layers), out_shape=s...]
where the time goes in v3:
time: 37.1 us; the launch traced here: 36.9 us
  Pallas kernels  36.3 us (98%)
  between operations  0.65 us (2%)
    pallas_call x1, Pallas kernels, shards(): pl.pallas_call(functools.partial(step_kernel, count, layers), out_shape=s...  31.1 us
    pallas_call x1, Pallas kernels, shards(): pl.pallas_call(result_kernel, out_shape=state, in_specs=[hbm] * 7, out_sp...  5.23 us

profile of v3, /device:TPU:0, one launch (start us, length us, event | category | flops | bytes accessed | tf_op | source)
XLA Modules:
  0.0 36.9 jit_solution(688628475444527052)
XLA Ops:
  0.6 31.1 %shard_map.198 = (f32[3,6,24,768]{3,2,1,0:T(8,128)}, f32[3,6,24,768]{3,2,1,0:T(8,128)}, f32[3,6,24,768]{3,2,1,0:T(8,128)}, f32[3,6,24,768]{3,2,1,0:T(8,128)}, f3...) custom-call(f32[3,6,24,768]{3,2,1,0:T(8,128)} %e_in.1, f32[3,6,24,768]{3,2,1,0:T(8,128)} %h_in.1, ...), custom_call_target="tpu_custom_call" | custom-call | tf_op jit(solution)/shard_map/pallas_call | solution.py:531
  31.7 5.2 %shard_map.199 = (f32[3,6,24,768]{3,2,1,0:T(8,128)}, f32[3,6,24,768]{3,2,1,0:T(8,128)}, f32[3,6,24,768]{3,2,1,0:T(8,128)}, f32[3,6,24,768]{3,2,1,0:T(8,128)}, f3...) custom-call(f32[3,6,24,768]{3,2,1,0:T(8,128)} %get-tuple-element.21.refs_0_, ...), custom_call_target="tpu_custom_call" | custom-call | tf_op jit(solution)/shard_map/pallas_call | solution.py:581
